TPU v7x, 32 devices: a whole 2x2x4 slice. The times are simulated.
32 devices in a mesh: groups: 2 (over x), chan: 16 (over z, y, core).
Axes of the slice: x: 2, y: 2, z: 4, core: 2. Of those that a mesh axis runs over, the one named last changes fastest.
Arguments:
- voltages: bfloat16 [4, 256, 16, 8192], P(None, 'chan', 'groups'), parts along dimension 2, may hold values from -3 to 3
- jones_terms: bfloat16 [16, 256, 8192], P('groups', 'chan'), parts along dimension 0, may hold values from -3 to 3
- rfi_flags: int32 [16, 8192], P('groups', 'chan'), parts along dimension 0, may hold values from 0 to 1, as said below
- delay_ticks: int32 [256, 256], replicated, may hold values from 0 to 8191
Outputs:
- beam_power: float32 [256, 16384], P('chan', 'groups'), parts along dimension 1
There are 2 independent parts, one for each index of `groups`. A program takes and returns all parts, laid end to end along the dimension named above; an argument that names none is the same for every part. Nothing has to cross between parts.
Inputs may be any that keep to these rules, and one draw needn't show every extreme that they name: `rfi_flags`: in every draw some channels are flagged at all 8 samples.
All inputs are finite; a program needn't handle non-finite values.
Results may differ from a plain program's by a relative error of at most 0.0017.
Values may be sent and summed in bfloat16 or wider, within the bound.
A program may use at most 256 MiB of HBM per device.

v0:
```python
import math

import jax
import jax.numpy as jnp
from jax import lax
from jax.sharding import PartitionSpec as P

STATIONS = 256
CHANNELS = 8192


def apply_jones(volt_block, jones_block):
    volt_parts = [volt_block[k].astype(jnp.float32) for k in range(4)]
    jones_parts = [jones_block[k].astype(jnp.float32) for k in range(8)]
    outputs = []
    for target in range(2):
        real_sum = jnp.zeros_like(volt_parts[0])
        imag_sum = jnp.zeros_like(volt_parts[0])
        for source in range(2):
            jones_re = jones_parts[4 * target + 2 * source]
            jones_im = jones_parts[4 * target + 2 * source + 1]
            volt_re = volt_parts[2 * source]
            volt_im = volt_parts[2 * source + 1]
            real_sum = real_sum + jones_re * volt_re - jones_im * volt_im
            imag_sum = imag_sum + jones_re * volt_im + jones_im * volt_re
        outputs.append(real_sum)
        outputs.append(imag_sum)
    return jnp.stack(outputs).astype(jnp.bfloat16)


def local(voltages, jones_terms, rfi_flags, delay_ticks):
    corrected_local = apply_jones(voltages, jones_terms[:, :, None, :])
    corrected = lax.all_to_all(corrected_local, "chan", split_axis=3, concat_axis=1, tiled=True)
    chan_dev = corrected.shape[3]
    block_width = math.gcd(32, chan_dev)
    block_total = chan_dev // block_width
    position = lax.axis_index("chan")
    weight_scale = 1.0 / math.sqrt(STATIONS)

    def one_block(first_chan):
        corr_block = lax.dynamic_slice_in_dim(corrected, first_chan, block_width, 3)
        flag_block = lax.dynamic_slice_in_dim(rfi_flags, first_chan, block_width, 1)
        chan_ids = position * chan_dev + first_chan + jnp.arange(block_width)
        turns = delay_ticks[None, :, :] * chan_ids[:, None, None] % CHANNELS
        phase_angle = turns.astype(jnp.float32) * (2.0 * math.pi / CHANNELS)
        weights = jnp.stack(
            [jnp.cos(phase_angle) * weight_scale, -jnp.sin(phase_angle) * weight_scale]
        ).astype(jnp.bfloat16)
        products = jnp.einsum(
            "wcbs,kstc->wkbtc", weights, corr_block, preferred_element_type=jnp.float32
        )
        x_re = products[0, 0] - products[1, 1]
        x_im = products[0, 1] + products[1, 0]
        y_re = products[0, 2] - products[1, 3]
        y_im = products[0, 3] + products[1, 2]
        sample_power = x_re * x_re + x_im * x_im + y_re * y_re + y_im * y_im
        kept_mask = (1 - flag_block).astype(jnp.float32)
        summed = jnp.sum(sample_power * kept_mask[None, :, :], axis=1)
        kept_count = jnp.sum(kept_mask, axis=0)
        return summed / jnp.maximum(kept_count, 1.0)[None, :]

    starts = jnp.arange(block_total) * block_width
    blocks = lax.map(one_block, starts)
    channel_power = jnp.moveaxis(blocks, 0, 1).reshape(blocks.shape[1], chan_dev)
    return lax.all_to_all(channel_power, "chan", split_axis=0, concat_axis=1, tiled=True)


def solution(mesh):
    return jax.shard_map(
        local,
        mesh=mesh,
        in_specs=(
            P(None, "chan", "groups", None),
            P("groups", "chan", None),
            P("groups", "chan"),
            P(),
        ),
        out_specs=P("chan", "groups"),
        check_vma=False,
    )
```

profile of v0, /device:TPU:0, one launch (start us, length us, event | category | flops | bytes accessed | tf_op | source)
XLA Modules:
  0.0 1164.9 jit_solution(13040302796680807438)
XLA Ops:
  14.0 55.7 %copy.33 = bf16[4,16,8,8192]{1,2,0,3:T(8,128)(2,1)} copy(bf16[4,16,8,8192]{3,2,1,0:T(8,128)(2,1)} %pad_maximum_fusion) | data formatting | bytes 16777216 | tf_op jit(solution)/shard_map/stack | solution.py:28
  69.7 72.4 %reshape.208 = bf16[16,2,131072]{2,1,0:T(2,128)(2,1)} reshape(bf16[8192,4,8,16]{3,2,1,0:T(8,128)(2,1)} %bitcast.58) | data formatting | bytes 16777216
  149.6 150.7 %all-to-all-done = bf16[16,2,131072]{2,1,0:T(2,128)(2,1)} async-done(((bf16[16,2,131072]{2,1,0:T(2,128)(2,1)}), bf16[16,2,131072]{2,1,0:T(2,128)(2,1)}, u32[]{:S(2)}, u32[]{:S(2)}) %all-to-all-start) | async-done | bytes 8388640 | tf_op jit(solution)/shard_map/all_to_all | solution.py:33
  300.3 48.5 %reshape.209 = bf16[8192,4,8,16]{3,2,1,0:T(8,128)(2,1)} reshape(bf16[16,2,131072]{2,1,0:T(2,128)(2,1)} %all-to-all-done) | data formatting | bytes 16777216
  348.8 69.9 %copy.35 = bf16[4,16,16,8,512]{4,3,2,1,0:T(8,128)(2,1)} copy(bf16[4,16,16,8,512]{2,3,0,4,1:T(8,128)(2,1)} %bitcast.18) | data formatting | bytes 16777216 | tf_op jit(solution)/shard_map/all_to_all | solution.py:33
  418.7 16.0 %copy.36 = bf16[4,256,8,512]{1,2,0,3:T(8,128)(2,1)} copy(bf16[4,256,8,512]{3,2,1,0:T(8,128)(2,1)} %bitcast.74) | data formatting | bytes 16777216 | tf_op jit(solution)/shard_map/while | solution.py:63
  434.7 676.4 %while.12 = (s32[]{:T(128)}, f32[16,256,32]{1,2,0:T(8,128)S(1)}, s32[16]{0:T(128)S(1)}, bf16[4,256,8,512]{1,2,0,3:T(8,128)(2,1)}, s32[256,256]{1,0:T(8,128)S(1)}...) while((s32[]{:T(128)}, f32[16,256,32]{1,2,0:T(8,128)S(1)}, s32[16]{0:T(128)S(1)}, ...), condition=%wide.region_3.4_spmd, body=%wide.region_0.3_spmd.sunk | while | flops 325911840 | bytes 21865776 | solution.py:63
  437.9 34.3 %multiply_convert_fusion.3 = (bf16[1,32,256,256]{3,2,0,1:T(8,128)(2,1)S(1)}, bf16[1,32,256,256]{3,2,0,1:T(8,128)(2,1)S(1)}) fusion(s32[32]{0:T(128)S(1)} %iota_add_fusion.2, s32[256,256]{1,0:T(8,128)S(1)} %get-tuple-element.232), kind=kLoop, calls=%fused_computation.13.clone.1 | loop fusion | flops 39845888 | bytes 8650880 | tf_op jit(solution)/shard_map/convert
  480.1 34.3 %multiply_convert_fusion.3 = (bf16[1,32,256,256]{3,2,0,1:T(8,128)(2,1)S(1)}, bf16[1,32,256,256]{3,2,0,1:T(8,128)(2,1)S(1)}) fusion(s32[32]{0:T(128)S(1)} %iota_add_fusion.2, s32[256,256]{1,0:T(8,128)S(1)} %get-tuple-element.232), kind=kLoop, calls=%fused_computation.13.clone.1 | loop fusion | flops 39845888 | bytes 8650880 | tf_op jit(solution)/shard_map/convert
  522.4 34.3 %multiply_convert_fusion.3 = (bf16[1,32,256,256]{3,2,0,1:T(8,128)(2,1)S(1)}, bf16[1,32,256,256]{3,2,0,1:T(8,128)(2,1)S(1)}) fusion(s32[32]{0:T(128)S(1)} %iota_add_fusion.2, s32[256,256]{1,0:T(8,128)S(1)} %get-tuple-element.232), kind=kLoop, calls=%fused_computation.13.clone.1 | loop fusion | flops 39845888 | bytes 8650880 | tf_op jit(solution)/shard_map/convert
  564.7 34.3 %multiply_convert_fusion.3 = (bf16[1,32,256,256]{3,2,0,1:T(8,128)(2,1)S(1)}, bf16[1,32,256,256]{3,2,0,1:T(8,128)(2,1)S(1)}) fusion(s32[32]{0:T(128)S(1)} %iota_add_fusion.2, s32[256,256]{1,0:T(8,128)S(1)} %get-tuple-element.232), kind=kLoop, calls=%fused_computation.13.clone.1 | loop fusion | flops 39845888 | bytes 8650880 | tf_op jit(solution)/shard_map/convert
  607.0 34.3 %multiply_convert_fusion.3 = (bf16[1,32,256,256]{3,2,0,1:T(8,128)(2,1)S(1)}, bf16[1,32,256,256]{3,2,0,1:T(8,128)(2,1)S(1)}) fusion(s32[32]{0:T(128)S(1)} %iota_add_fusion.2, s32[256,256]{1,0:T(8,128)S(1)} %get-tuple-element.232), kind=kLoop, calls=%fused_computation.13.clone.1 | loop fusion | flops 39845888 | bytes 8650880 | tf_op jit(solution)/shard_map/convert
  649.3 34.3 %multiply_convert_fusion.3 = (bf16[1,32,256,256]{3,2,0,1:T(8,128)(2,1)S(1)}, bf16[1,32,256,256]{3,2,0,1:T(8,128)(2,1)S(1)}) fusion(s32[32]{0:T(128)S(1)} %iota_add_fusion.2, s32[256,256]{1,0:T(8,128)S(1)} %get-tuple-element.232), kind=kLoop, calls=%fused_computation.13.clone.1 | loop fusion | flops 39845888 | bytes 8650880 | tf_op jit(solution)/shard_map/convert
  691.5 34.3 %multiply_convert_fusion.3 = (bf16[1,32,256,256]{3,2,0,1:T(8,128)(2,1)S(1)}, bf16[1,32,256,256]{3,2,0,1:T(8,128)(2,1)S(1)}) fusion(s32[32]{0:T(128)S(1)} %iota_add_fusion.2, s32[256,256]{1,0:T(8,128)S(1)} %get-tuple-element.232), kind=kLoop, calls=%fused_computation.13.clone.1 | loop fusion | flops 39845888 | bytes 8650880 | tf_op jit(solution)/shard_map/convert
  733.8 34.3 %multiply_convert_fusion.3 = (bf16[1,32,256,256]{3,2,0,1:T(8,128)(2,1)S(1)}, bf16[1,32,256,256]{3,2,0,1:T(8,128)(2,1)S(1)}) fusion(s32[32]{0:T(128)S(1)} %iota_add_fusion.2, s32[256,256]{1,0:T(8,128)S(1)} %get-tuple-element.232), kind=kLoop, calls=%fused_computation.13.clone.1 | loop fusion | flops 39845888 | bytes 8650880 | tf_op jit(solution)/shard_map/convert
  776.1 34.3 %multiply_convert_fusion.3 = (bf16[1,32,256,256]{3,2,0,1:T(8,128)(2,1)S(1)}, bf16[1,32,256,256]{3,2,0,1:T(8,128)(2,1)S(1)}) fusion(s32[32]{0:T(128)S(1)} %iota_add_fusion.2, s32[256,256]{1,0:T(8,128)S(1)} %get-tuple-element.232), kind=kLoop, calls=%fused_computation.13.clone.1 | loop fusion | flops 39845888 | bytes 8650880 | tf_op jit(solution)/shard_map/convert
  818.4 34.3 %multiply_convert_fusion.3 = (bf16[1,32,256,256]{3,2,0,1:T(8,128)(2,1)S(1)}, bf16[1,32,256,256]{3,2,0,1:T(8,128)(2,1)S(1)}) fusion(s32[32]{0:T(128)S(1)} %iota_add_fusion.2, s32[256,256]{1,0:T(8,128)S(1)} %get-tuple-element.232), kind=kLoop, calls=%fused_computation.13.clone.1 | loop fusion | flops 39845888 | bytes 8650880 | tf_op jit(solution)/shard_map/convert
  860.7 34.3 %multiply_convert_fusion.3 = (bf16[1,32,256,256]{3,2,0,1:T(8,128)(2,1)S(1)}, bf16[1,32,256,256]{3,2,0,1:T(8,128)(2,1)S(1)}) fusion(s32[32]{0:T(128)S(1)} %iota_add_fusion.2, s32[256,256]{1,0:T(8,128)S(1)} %get-tuple-element.232), kind=kLoop, calls=%fused_computation.13.clone.1 | loop fusion | flops 39845888 | bytes 8650880 | tf_op jit(solution)/shard_map/convert
  902.9 34.3 %multiply_convert_fusion.3 = (bf16[1,32,256,256]{3,2,0,1:T(8,128)(2,1)S(1)}, bf16[1,32,256,256]{3,2,0,1:T(8,128)(2,1)S(1)}) fusion(s32[32]{0:T(128)S(1)} %iota_add_fusion.2, s32[256,256]{1,0:T(8,128)S(1)} %get-tuple-element.232), kind=kLoop, calls=%fused_computation.13.clone.1 | loop fusion | flops 39845888 | bytes 8650880 | tf_op jit(solution)/shard_map/convert
  945.2 34.3 %multiply_convert_fusion.3 = (bf16[1,32,256,256]{3,2,0,1:T(8,128)(2,1)S(1)}, bf16[1,32,256,256]{3,2,0,1:T(8,128)(2,1)S(1)}) fusion(s32[32]{0:T(128)S(1)} %iota_add_fusion.2, s32[256,256]{1,0:T(8,128)S(1)} %get-tuple-element.232), kind=kLoop, calls=%fused_computation.13.clone.1 | loop fusion | flops 39845888 | bytes 8650880 | tf_op jit(solution)/shard_map/convert
  987.5 34.3 %multiply_convert_fusion.3 = (bf16[1,32,256,256]{3,2,0,1:T(8,128)(2,1)S(1)}, bf16[1,32,256,256]{3,2,0,1:T(8,128)(2,1)S(1)}) fusion(s32[32]{0:T(128)S(1)} %iota_add_fusion.2, s32[256,256]{1,0:T(8,128)S(1)} %get-tuple-element.232), kind=kLoop, calls=%fused_computation.13.clone.1 | loop fusion | flops 39845888 | bytes 8650880 | tf_op jit(solution)/shard_map/convert
  1029.8 34.3 %multiply_convert_fusion.3 = (bf16[1,32,256,256]{3,2,0,1:T(8,128)(2,1)S(1)}, bf16[1,32,256,256]{3,2,0,1:T(8,128)(2,1)S(1)}) fusion(s32[32]{0:T(128)S(1)} %iota_add_fusion.2, s32[256,256]{1,0:T(8,128)S(1)} %get-tuple-element.232), kind=kLoop, calls=%fused_computation.13.clone.1 | loop fusion | flops 39845888 | bytes 8650880 | tf_op jit(solution)/shard_map/convert
  1072.0 34.3 %multiply_convert_fusion.3 = (bf16[1,32,256,256]{3,2,0,1:T(8,128)(2,1)S(1)}, bf16[1,32,256,256]{3,2,0,1:T(8,128)(2,1)S(1)}) fusion(s32[32]{0:T(128)S(1)} %iota_add_fusion.2, s32[256,256]{1,0:T(8,128)S(1)} %get-tuple-element.232), kind=kLoop, calls=%fused_computation.13.clone.1 | loop fusion | flops 39845888 | bytes 8650880 | tf_op jit(solution)/shard_map/convert
  1113.3 50.8 %all_to_all.37 = f32[16,16,512]{2,1,0:T(8,128)S(1)} all-to-all(f32[16,16,512]{2,1,0:T(8,128)S(1)} %all_to_all.31), channel_id=1, replica_groups=mesh['groups'=2,'chan'=16] {'chan'}, dimensions={0} | all-to-all | bytes 1048576 | tf_op jit(solution)/shard_map/all_to_all | solution.py:65
  (177 shorter events, 111.0 us)
Async XLA Ops:
  0.0 7.4 slice-start
  2.1 5.3 slice-start.1
  142.1 158.2 %all-to-all-start = ((bf16[16,2,131072]{2,1,0:T(2,128)(2,1)}), bf16[16,2,131072]{2,1,0:T(2,128)(2,1)}, u32[]{:S(2)}, u32[]{:S(2)}) async-start(bf16[16,2,131072]{2,1,0:T(2,128)(2,1)} %reshape.208), calls=%async_computation | async-start | bytes 16777216 | tf_op jit(solution)/shard_map/all_to_all | solution.py:33
  418.7 16.0 %copy-start = (s32[256,256]{1,0:T(8,128)S(1)}, s32[256,256]{1,0:T(8,128)}, u32[]{:S(2)}) copy-start(s32[256,256]{1,0:T(8,128)} %param.9) | copy-start | bytes 786436
where the time goes:
time: 1170 us; the launch traced here: 1160 us
  other arithmetic  569 us (49%)
  local copies, waits for them, and re-layouts  289 us (25%)
  waiting for transfers between devices  151 us (13%)
  matrix products  56.9 us (5%)
  blocking collectives  50.8 us (4%)
  loops' own time  41.1 us (4%)
    another operation x18, other arithmetic  557 us
    all_to_all x1, waiting for transfers between devices, local(): lax.all_to_all(corrected_local, 'chan', split_axis=3, concat_axis=1, tile...  151 us
    unnamed x8, local copies, waits for them, and re-layouts  121 us
    all_to_all x1, local copies, waits for them, and re-layouts, local(): lax.all_to_all(corrected_local, 'chan', split_axis=3, concat_axis=1, tile...  69.9 us
    dot_general x16, matrix products, one_block(): jnp.einsum('wcbs,kstc->wkbtc', weights, corr_block, preferred_element_typ...  56.9 us
    another operation x1, local copies, waits for them, and re-layouts, apply_jones(): return jnp.stack(outputs).astype(jnp.bfloat16)  55.7 us
    all_to_all x1, blocking collectives, local(): lax.all_to_all(channel_power, 'chan', split_axis=0, concat_axis=1, tiled=...  50.8 us
    another operation x1, loops' own time, local(): blocks = lax.map(one_block, starts)  41.1 us
  transfers between devices with their start and end apart: 1, of which 1 were waited for; matrix products, arithmetic and copies ran while one was open for 0% of the time, Pallas kernels for 0%

commit v1 on v0

v1 whole, which is shorter than its diff:
```python
import functools
import math

import jax
import jax.numpy as jnp
from jax import lax
from jax.experimental import pallas as pl
from jax.experimental.pallas import tpu as pltpu
from jax.sharding import PartitionSpec as P

LANES = 128
PAIRS = 8


def kernel(dims, volt_hbm, jones_hbm, flags, ticks, out, volt, jones, jones_f, send, recv, wide,
           turned, base, table, power, out_send, out_recv, volt_sem, jones_sem,
           send_sem, recv_sem, osend_sem, orecv_sem):
    n, s_loc, tsamp, chunks, beams, stations, channels = dims
    rows = 4 * tsamp
    width = chunks * LANES
    b_loc = beams // n
    me = lax.axis_index("chan")

    def partner(i):
        step = (i + 1) // 2
        off = n // 2 + jnp.where(i % 2 == 1, -step, step)
        return lax.rem(me + off + n, n)

    def load(j):
        cols = pl.ds(pl.multiple_of(j * width, LANES), width)
        return (
            pltpu.make_async_copy(volt_hbm.at[:, cols], volt.at[:, cols], volt_sem.at[j]),
            pltpu.make_async_copy(jones_hbm.at[:, cols], jones.at[:, cols], jones_sem.at[j]),
        )

    @pl.loop(0, n)
    def _(i):
        for copy in load(partner(i)):
            copy.start()

    barrier = pltpu.get_barrier_semaphore()

    @pl.loop(0, n - 1)
    def _(i):
        pl.semaphore_signal(barrier, inc=1, device_id={"chan": partner(i)},
                            device_id_type=pl.DeviceIdType.MESH)

    pl.semaphore_wait(barrier, n - 1)

    def volt_copy(q, j, origin):
        return pltpu.make_async_remote_copy(
            src_ref=send.at[q, j], dst_ref=recv.at[q, origin],
            send_sem=send_sem.at[q, j], recv_sem=recv_sem.at[q, origin],
            device_id={"chan": j}, device_id_type=pl.DeviceIdType.MESH)

    def power_copy(q, j, origin):
        return pltpu.make_async_remote_copy(
            src_ref=out_send.at[q, j], dst_ref=out_recv.at[q, origin],
            send_sem=osend_sem.at[q, j], recv_sem=orecv_sem.at[q, origin],
            device_id={"chan": j}, device_id_type=pl.DeviceIdType.MESH)

    def correct(q, j, put):
        cols = pl.ds(pl.multiple_of(j * width + q * LANES, LANES), LANES)
        jones_f[...] = jones[:, cols].astype(jnp.float32)
        for s in range(0, s_loc, 2):
            v = [volt[pl.ds(k * s_loc * tsamp + s * tsamp, 2 * tsamp), cols].astype(jnp.float32)
                 for k in range(4)]
            for e in range(2):
                ve = [a[e * tsamp:(e + 1) * tsamp] for a in v]
                m = [jnp.broadcast_to(jones_f[pl.ds(i * s_loc + s + e, 1), :], (tsamp, LANES))
                     for i in range(8)]
                done = []
                for o in range(2):
                    r0, i0, r1, i1 = m[4 * o:4 * o + 4]
                    done.append(r0 * ve[0] - i0 * ve[1] + r1 * ve[2] - i1 * ve[3])
                    done.append(r0 * ve[1] + i0 * ve[0] + r1 * ve[3] + i1 * ve[2])
                put(s + e, jnp.concatenate(done, axis=0).astype(jnp.bfloat16))

    @pl.loop(0, chunks)
    def _(q):
        @pl.loop(0, n)
        def _(i):
            j = partner(i)

            @pl.when(q == 0)
            def _():
                for copy in load(j):
                    copy.wait()

            def put(s, value):
                send[q, j, s] = value

            correct(q, j, put)

            @pl.when(i < n - 1)
            def _():
                volt_copy(q, j, me).start()

    scale = 1.0 / math.sqrt(stations)

    def turn(part, twice):
        t = lax.rem(part * twice, 2 * channels)
        t = jnp.where(t >= channels, t - 2 * channels, t)
        angle = t.astype(jnp.float32) * (math.pi / channels)
        return jnp.cos(angle), -jnp.sin(angle)

    def mul(a, b):
        return a[0] * b[0] - a[1] * b[1], a[0] * b[1] + a[1] * b[0]

    @pl.loop(0, stations // 16)
    def _(i):
        at = pl.ds(pl.multiple_of(i * 16, 16), 16)
        part = ticks[at, :]
        first = turn(part, me * (2 * width) + 2 * PAIRS - 1)
        base[0, at, :] = first[0] * scale
        base[1, at, :] = first[1] * scale
        jump = turn(part, 4 * PAIRS)
        table[PAIRS, 0, at, :] = jump[0]
        table[PAIRS, 1, at, :] = jump[1]
        half = turn(part, 1)
        one = turn(part, 2)
        for k in range(PAIRS):
            table[k, 0, at, :] = half[0]
            table[k, 1, at, :] = half[1]
            half = mul(half, one)

    @pl.loop(0, chunks)
    def _(q):
        @pl.loop(0, n - 1)
        def _(i):
            volt_copy(q, partner(i), partner(i)).wait_recv()

        kept = (1 - flags[:, pl.ds(pl.multiple_of(q * LANES, LANES), LANES)]).astype(jnp.float32)
        mask = jnp.concatenate([kept] * 4, axis=0)

        def widen(j, ref):
            @pl.loop(0, s_loc // 2)
            def _(s):
                for e in range(2):
                    at = pl.multiple_of((j * s_loc + 2 * s + e) * rows, rows)
                    wide[pl.ds(at, rows), :] = ref[2 * s + e].astype(jnp.float32) * mask

        @pl.loop(0, n - 1)
        def _(i):
            j = partner(i)
            widen(j, recv.at[q, j])

        widen(me, send.at[q, me])

        halves = stations // LANES

        @pl.loop(0, rows)
        def _(r):
            for h in range(halves):
                got = wide[pl.ds(h * LANES * rows + r, LANES, stride=rows), :]
                turned[h, pl.ds(r, LANES, stride=rows), :] = got.T

        @pl.loop(0, LANES // (2 * PAIRS))
        def _(g):
            @pl.loop(0, PAIRS)
            def _(k):
                a, b = base[0], base[1]
                c, d = table[k, 0], table[k, 1]
                ac, bd, ad, bc = a * c, b * d, a * d, b * c
                for up in (True, False):
                    if up:
                        wr, wi, chan = ac - bd, ad + bc, g * (2 * PAIRS) + PAIRS + k
                    else:
                        wr, wi, chan = ac + bd, bc - ad, g * (2 * PAIRS) + PAIRS - 1 - k
                    at = pl.ds(pl.multiple_of(chan * rows, rows), rows)
                    x = jnp.concatenate([turned[h, at, :] for h in range(halves)], axis=1)
                    y = jnp.concatenate([-x[tsamp:2 * tsamp], x[:tsamp],
                                         -x[3 * tsamp:], x[2 * tsamp:3 * tsamp]], axis=0)
                    z = jnp.dot(x.astype(jnp.bfloat16), wr.astype(jnp.bfloat16),
                                preferred_element_type=jnp.float32)
                    z += jnp.dot(y.astype(jnp.bfloat16), wi.astype(jnp.bfloat16),
                                 preferred_element_type=jnp.float32)
                    power[pl.ds(chan, 1), :] = jnp.sum(z * z, axis=0, keepdims=True)

            @pl.loop(0, stations // 16)
            def _(i):
                at = pl.ds(pl.multiple_of(i * 16, 16), 16)
                moved = mul((base[0, at, :], base[1, at, :]),
                            (table[PAIRS, 0, at, :], table[PAIRS, 1, at, :]))
                base[0, at, :] = moved[0]
                base[1, at, :] = moved[1]

        count = jnp.maximum(jnp.sum(kept, axis=0, keepdims=True), 1.0)
        result = power[...].T / count
        for j in range(n):
            out_send[q, j, 0:b_loc, :] = result[j * b_loc:(j + 1) * b_loc]

        @pl.loop(0, n - 1)
        def _(i):
            power_copy(q, partner(i), me).start()

    @pl.loop(0, chunks)
    def _(q):
        out[:, pl.ds(pl.multiple_of(me * width + q * LANES, LANES), LANES)] = out_send[q, me, 0:b_loc, :]

        @pl.loop(0, n - 1)
        def _(i):
            j = partner(i)
            power_copy(q, j, j).wait_recv()
            out[:, pl.ds(pl.multiple_of(j * width + q * LANES, LANES), LANES)] = out_recv[q, j, 0:b_loc, :]
            power_copy(q, j, me).wait_send()
            volt_copy(q, j, me).wait_send()


def local(n, voltages, jones_terms, rfi_flags, delay_ticks):
    _, s_loc, tsamp, channels = voltages.shape
    beams, stations = delay_ticks.shape
    chunks = channels // n // LANES
    b_loc = beams // n
    b_pad = -(-b_loc // 8) * 8
    rows = 4 * tsamp
    dims = (n, s_loc, tsamp, chunks, beams, stations, channels)
    f32, bf16 = jnp.float32, jnp.bfloat16
    anywhere = pl.BlockSpec(memory_space=pl.ANY)
    vmem = pl.BlockSpec(memory_space=pltpu.VMEM)
    dma = pltpu.SemaphoreType.DMA
    return pl.pallas_call(
        functools.partial(kernel, dims),
        out_shape=jax.ShapeDtypeStruct((b_loc, channels), f32),
        in_specs=[anywhere, anywhere, vmem, vmem],
        out_specs=vmem,
        scratch_shapes=[
            pltpu.VMEM((4 * s_loc * tsamp, channels), bf16),
            pltpu.VMEM((8 * s_loc, channels), bf16),
            pltpu.VMEM((8 * s_loc, LANES), f32),
            pltpu.VMEM((chunks, n, s_loc, rows, LANES), bf16),
            pltpu.VMEM((chunks, n, s_loc, rows, LANES), bf16),
            pltpu.VMEM((stations * rows, LANES), f32),
            pltpu.VMEM((stations // LANES, LANES * rows, LANES), f32),
            pltpu.VMEM((2, stations, beams), f32),
            pltpu.VMEM((PAIRS + 1, 2, stations, beams), f32),
            pltpu.VMEM((LANES, beams), f32),
            pltpu.VMEM((chunks, n, b_pad, LANES), f32),
            pltpu.VMEM((chunks, n, b_pad, LANES), f32),
            dma((n,)), dma((n,)),
            dma((chunks, n)), dma((chunks, n)), dma((chunks, n)), dma((chunks, n)),
        ],
        compiler_params=pltpu.CompilerParams(
            collective_id=0, has_side_effects=True, vmem_limit_bytes=56 * 1024 * 1024),
    )(
        voltages.reshape(4 * s_loc * tsamp, channels),
        jones_terms.reshape(8 * s_loc, channels),
        rfi_flags,
        delay_ticks.T,
    )


def solution(mesh):
    return jax.shard_map(
        functools.partial(local, mesh.shape["chan"]),
        mesh=mesh,
        in_specs=(
            P(None, "chan", "groups", None),
            P("groups", "chan", None),
            P("groups", "chan"),
            P(),
        ),
        out_specs=P("chan", "groups"),
        check_vma=False,
    )
```

time: 1170 us -> 238 us (0.20)
  other arithmetic: 569 us -> 0 us
  local copies, waits for them, and re-layouts: 289 us -> 3.65 us
  Pallas kernels: 0 us -> 234 us
  waiting for transfers between devices: 151 us -> 0 us
  matrix products: 56.9 us -> 0 us
  blocking collectives: 50.8 us -> 0 us
  loops' own time: 41.1 us -> 0 us
    another operation x19 -> x0, other arithmetic: 561 us -> none
    pallas_call x0 -> x1, Pallas kernels: none -> 234 us  [local(): pl.pallas_call(functools.partial(kernel, dims), out_shape=jax.ShapeDtypeS...]
    all_to_all x1 -> x0, waiting for transfers between devices: 151 us -> none  [local(): lax.all_to_all(corrected_local, 'chan', split_axis=3, concat_axis=1, tile...]
    unnamed x8 -> x2, local copies, waits for them, and re-layouts: 121 us -> 3.65 us
    all_to_all x3 -> x0, local copies, waits for them, and re-layouts: 71.5 us -> none  [the longest x1 69.9 us: local(): lax.all_to_all(corrected_local, 'chan', split_axis=3, concat_axis=1, tile...]
    dot_general x16 -> x0, matrix products: 56.9 us -> none  [one_block(): jnp.einsum('wcbs,kstc->wkbtc', weights, corr_block, preferred_element_typ...]
    another operation x1 -> x0, local copies, waits for them, and re-layouts: 55.7 us -> none  [apply_jones(): return jnp.stack(outputs).astype(jnp.bfloat16)]
    all_to_all x1 -> x0, blocking collectives: 50.8 us -> none  [local(): lax.all_to_all(channel_power, 'chan', split_axis=0, concat_axis=1, tiled=...]
  transfers between devices with their start and end apart: 1 -> 0, of which waited for: 1 -> 0; matrix products, arithmetic and copies ran while one was open for 0% -> 0% of each run, Pallas kernels for 0% -> 0%
where the time goes in v1:
time: 238 us
  Pallas kernels  234 us (98%)
  local copies, waits for them, and re-layouts  3.65 us (2%)
    pallas_call x1, Pallas kernels, local(): pl.pallas_call(functools.partial(kernel, dims), out_shape=jax.ShapeDtypeS...  234 us

profile of v1, /device:TPU:0, one launch (start us, length us, event | category | flops | bytes accessed | tf_op | source)
XLA Modules:
  0.0 238.0 jit_solution(2628725457791891479)
XLA Ops:
  0.0 1.8 copy.5
  1.8 234.3 %shard_map.46 = f32[16,8192]{1,0:T(8,128)} custom-call(bf16[512,8192]{1,0:T(8,128)(2,1)} %bitcast.3, bf16[128,8192]{1,0:T(8,128)(2,1)} %bitcast.4, s32[8,512]{1,0:T(8,128)} %flags.1, s32[256,256]{1,0:T(8,128)} %bitcast.5), custom_call_target="tpu_custom_call" | custom-call | tf_op jit(solution)/shard_map/pallas_call | solution.py:222
  236.1 1.9 copy.7

commit v2 on v1

--- a/solution.py
+++ b/solution.py
@@ -10,21 +10,25 @@
 
 LANES = 128
 PAIRS = 8
+PITCH = 40
+UNROLL = 8
 
 
 def kernel(dims, volt_hbm, jones_hbm, flags, ticks, out, volt, jones, jones_f, send, recv, wide,
-           turned, base, table, power, out_send, out_recv, volt_sem, jones_sem,
+           turned, ticks_t, partial, base, table, power, out_send, out_recv, volt_sem, jones_sem,
            send_sem, recv_sem, osend_sem, orecv_sem):
     n, s_loc, tsamp, chunks, beams, stations, channels = dims
     rows = 4 * tsamp
     width = chunks * LANES
     b_loc = beams // n
     me = lax.axis_index("chan")
+    half = n // 2
+    side, place = me // half, lax.rem(me, half)
 
     def partner(i):
         step = (i + 1) // 2
-        off = n // 2 + jnp.where(i % 2 == 1, -step, step)
-        return lax.rem(me + off + n, n)
+        return jnp.where(i % 2 == 0, (1 - side) * half + lax.rem(place + step, half),
+                         side * half + lax.rem(place + step, half))
 
     def load(j):
         cols = pl.ds(pl.multiple_of(j * width, LANES), width)
@@ -33,17 +37,17 @@
             pltpu.make_async_copy(jones_hbm.at[:, cols], jones.at[:, cols], jones_sem.at[j]),
         )
 
+    barrier = pltpu.get_barrier_semaphore()
+
+    @pl.loop(0, n - 1)
+    def _(i):
+        pl.semaphore_signal(barrier, inc=1, device_id={"chan": partner(i)},
+                            device_id_type=pl.DeviceIdType.MESH)
+
     @pl.loop(0, n)
     def _(i):
         for copy in load(partner(i)):
             copy.start()
-
-    barrier = pltpu.get_barrier_semaphore()
-
-    @pl.loop(0, n - 1)
-    def _(i):
-        pl.semaphore_signal(barrier, inc=1, device_id={"chan": partner(i)},
-                            device_id_type=pl.DeviceIdType.MESH)
 
     pl.semaphore_wait(barrier, n - 1)
 
@@ -107,10 +111,12 @@
     def mul(a, b):
         return a[0] * b[0] - a[1] * b[1], a[0] * b[1] + a[1] * b[0]
 
+    ticks_t[...] = ticks[...].T
+
     @pl.loop(0, stations // 16)
     def _(i):
         at = pl.ds(pl.multiple_of(i * 16, 16), 16)
-        part = ticks[at, :]
+        part = ticks_t[at, :]
         first = turn(part, me * (2 * width) + 2 * PAIRS - 1)
         base[0, at, :] = first[0] * scale
         base[1, at, :] = first[1] * scale
@@ -124,67 +130,73 @@
             table[k, 1, at, :] = half[1]
             half = mul(half, one)
 
-    @pl.loop(0, chunks)
-    def _(q):
-        @pl.loop(0, n - 1)
-        def _(i):
-            volt_copy(q, partner(i), partner(i)).wait_recv()
-
+    def gather(q, h, own):
         kept = (1 - flags[:, pl.ds(pl.multiple_of(q * LANES, LANES), LANES)]).astype(jnp.float32)
         mask = jnp.concatenate([kept] * 4, axis=0)
 
         def widen(j, ref):
-            @pl.loop(0, s_loc // 2)
+            @pl.loop(0, s_loc, unroll=min(s_loc, 8))
             def _(s):
-                for e in range(2):
-                    at = pl.multiple_of((j * s_loc + 2 * s + e) * rows, rows)
-                    wide[pl.ds(at, rows), :] = ref[2 * s + e].astype(jnp.float32) * mask
-
-        @pl.loop(0, n - 1)
-        def _(i):
-            j = partner(i)
+                at = pl.multiple_of((lax.rem(j, half) * s_loc + s) * PITCH, 8)
+                wide[pl.ds(at, rows), :] = ref[s].astype(jnp.float32) * mask
+
+        @pl.loop(0, half - 1 if own else half)
+        def _(i):
+            j = h * half + lax.rem(place + (i + 1 if own else i), half)
+            volt_copy(q, j, j).wait_recv()
             widen(j, recv.at[q, j])
 
-        widen(me, send.at[q, me])
-
-        halves = stations // LANES
-
-        @pl.loop(0, rows)
+        if own:
+            widen(me, send.at[q, me])
+
+        @pl.loop(0, rows, unroll=4)
         def _(r):
-            for h in range(halves):
-                got = wide[pl.ds(h * LANES * rows + r, LANES, stride=rows), :]
-                turned[h, pl.ds(r, LANES, stride=rows), :] = got.T
+            got = wide[pl.ds(r, LANES, stride=PITCH), :]
+            turned[pl.ds(r, LANES, stride=PITCH), :] = got.T
+
+    def combine(h, own):
+        members = pl.ds(pl.multiple_of(h * LANES, LANES), LANES)
 
         @pl.loop(0, LANES // (2 * PAIRS))
         def _(g):
-            @pl.loop(0, PAIRS)
+            @pl.loop(0, PAIRS, unroll=UNROLL)
             def _(k):
-                a, b = base[0], base[1]
-                c, d = table[k, 0], table[k, 1]
+                a, b = base[0, members, :], base[1, members, :]
+                c, d = table[k, 0, members, :], table[k, 1, members, :]
                 ac, bd, ad, bc = a * c, b * d, a * d, b * c
                 for up in (True, False):
                     if up:
                         wr, wi, chan = ac - bd, ad + bc, g * (2 * PAIRS) + PAIRS + k
                     else:
                         wr, wi, chan = ac + bd, bc - ad, g * (2 * PAIRS) + PAIRS - 1 - k
-                    at = pl.ds(pl.multiple_of(chan * rows, rows), rows)
-                    x = jnp.concatenate([turned[h, at, :] for h in range(halves)], axis=1)
+                    x = turned[pl.ds(pl.multiple_of(chan * PITCH, 8), rows), :]
                     y = jnp.concatenate([-x[tsamp:2 * tsamp], x[:tsamp],
                                          -x[3 * tsamp:], x[2 * tsamp:3 * tsamp]], axis=0)
-                    z = jnp.dot(x.astype(jnp.bfloat16), wr.astype(jnp.bfloat16),
+                    w = jnp.concatenate([wr.astype(jnp.bfloat16), wi.astype(jnp.bfloat16)], axis=0)
+                    z = jnp.dot(jnp.concatenate([x, y], axis=1).astype(jnp.bfloat16), w,
                                 preferred_element_type=jnp.float32)
-                    z += jnp.dot(y.astype(jnp.bfloat16), wi.astype(jnp.bfloat16),
-                                 preferred_element_type=jnp.float32)
-                    power[pl.ds(chan, 1), :] = jnp.sum(z * z, axis=0, keepdims=True)
-
-            @pl.loop(0, stations // 16)
+                    at = pl.ds(pl.multiple_of(chan * rows, rows), rows)
+                    if own:
+                        partial[at, :] = z
+                    else:
+                        z += partial[at, :]
+                        power[pl.ds(chan, 1), :] = jnp.sum(z * z, axis=0, keepdims=True)
+
+            @pl.loop(0, LANES // 16)
             def _(i):
-                at = pl.ds(pl.multiple_of(i * 16, 16), 16)
+                at = pl.ds(pl.multiple_of(h * LANES + i * 16, 16), 16)
                 moved = mul((base[0, at, :], base[1, at, :]),
                             (table[PAIRS, 0, at, :], table[PAIRS, 1, at, :]))
                 base[0, at, :] = moved[0]
                 base[1, at, :] = moved[1]
 
+    @pl.loop(0, chunks)
+    def _(q):
+        gather(q, side, True)
+        combine(side, True)
+        gather(q, 1 - side, False)
+        combine(1 - side, False)
+        kept = (1 - flags[:, pl.ds(pl.multiple_of(q * LANES, LANES), LANES)]).astype(jnp.float32)
         count = jnp.maximum(jnp.sum(kept, axis=0, keepdims=True), 1.0)
         result = power[...].T / count
         for j in range(n):
@@ -230,8 +242,10 @@
             pltpu.VMEM((8 * s_loc, LANES), f32),
             pltpu.VMEM((chunks, n, s_loc, rows, LANES), bf16),
             pltpu.VMEM((chunks, n, s_loc, rows, LANES), bf16),
-            pltpu.VMEM((stations * rows, LANES), f32),
-            pltpu.VMEM((stations // LANES, LANES * rows, LANES), f32),
+            pltpu.VMEM((LANES * PITCH, LANES), f32),
+            pltpu.VMEM((LANES * PITCH, LANES), f32),
+            pltpu.VMEM((stations, beams), jnp.int32),
+            pltpu.VMEM((LANES * rows, beams), f32),
             pltpu.VMEM((2, stations, beams), f32),
             pltpu.VMEM((PAIRS + 1, 2, stations, beams), f32),
             pltpu.VMEM((LANES, beams), f32),
@@ -246,7 +260,7 @@
         voltages.reshape(4 * s_loc * tsamp, channels),
         jones_terms.reshape(8 * s_loc, channels),
         rfi_flags,
-        delay_ticks.T,
+        delay_ticks,
     )
 
 

time: 238 us -> 210 us (0.88)
  Pallas kernels: 234 us -> 208 us
    pallas_call x1, Pallas kernels: 234 us -> 208 us  [local(): pl.pallas_call(functools.partial(kernel, dims), out_shape=jax.ShapeDtypeS...]
where the time goes in v2:
time: 210 us
  Pallas kernels  208 us (99%)
    pallas_call x1, Pallas kernels, local(): pl.pallas_call(functools.partial(kernel, dims), out_shape=jax.ShapeDtypeS...  208 us

profile of v2, /device:TPU:0, one launch (start us, length us, event | category | flops | bytes accessed | tf_op | source)
XLA Modules:
  0.0 210.1 jit_solution(17385458416664771977)
XLA Ops:
  0.0 208.2 %shard_map.46 = f32[16,8192]{1,0:T(8,128)} custom-call(bf16[512,8192]{1,0:T(8,128)(2,1)} %bitcast.2, bf16[128,8192]{1,0:T(8,128)(2,1)} %bitcast.3, s32[8,512]{1,0:T(8,128)} %flags.1, s32[256,256]{1,0:T(8,128)} %ticks.1), custom_call_target="tpu_custom_call" | custom-call | tf_op jit(solution)/shard_map/pallas_call | solution.py:234
  208.2 1.9 copy.6

commit v3 on v2

--- a/solution.py
+++ b/solution.py
@@ -200,7 +200,7 @@
         count = jnp.maximum(jnp.sum(kept, axis=0, keepdims=True), 1.0)
         result = power[...].T / count
         for j in range(n):
-            out_send[q, j, 0:b_loc, :] = result[j * b_loc:(j + 1) * b_loc]
+            out_send[q, j, 0:b_loc, :] = result[j * b_loc:(j + 1) * b_loc].astype(jnp.bfloat16)
 
         @pl.loop(0, n - 1)
         def _(i):
@@ -208,13 +208,13 @@
 
     @pl.loop(0, chunks)
     def _(q):
-        out[:, pl.ds(pl.multiple_of(me * width + q * LANES, LANES), LANES)] = out_send[q, me, 0:b_loc, :]
+        out[:, pl.ds(pl.multiple_of(me * width + q * LANES, LANES), LANES)] = out_send[q, me, 0:b_loc, :].astype(jnp.float32)
 
         @pl.loop(0, n - 1)
         def _(i):
             j = partner(i)
             power_copy(q, j, j).wait_recv()
-            out[:, pl.ds(pl.multiple_of(j * width + q * LANES, LANES), LANES)] = out_recv[q, j, 0:b_loc, :]
+            out[:, pl.ds(pl.multiple_of(j * width + q * LANES, LANES), LANES)] = out_recv[q, j, 0:b_loc, :].astype(jnp.float32)
             power_copy(q, j, me).wait_send()
             volt_copy(q, j, me).wait_send()
 
@@ -224,7 +224,7 @@
     beams, stations = delay_ticks.shape
     chunks = channels // n // LANES
     b_loc = beams // n
-    b_pad = -(-b_loc // 8) * 8
+    b_pad = -(-b_loc // 16) * 16
     rows = 4 * tsamp
     dims = (n, s_loc, tsamp, chunks, beams, stations, channels)
     f32, bf16 = jnp.float32, jnp.bfloat16
@@ -249,8 +249,8 @@
             pltpu.VMEM((2, stations, beams), f32),
             pltpu.VMEM((PAIRS + 1, 2, stations, beams), f32),
             pltpu.VMEM((LANES, beams), f32),
-            pltpu.VMEM((chunks, n, b_pad, LANES), f32),
-            pltpu.VMEM((chunks, n, b_pad, LANES), f32),
+            pltpu.VMEM((chunks, n, b_pad, LANES), bf16),
+            pltpu.VMEM((chunks, n, b_pad, LANES), bf16),
             dma((n,)), dma((n,)),
             dma((chunks, n)), dma((chunks, n)), dma((chunks, n)), dma((chunks, n)),
         ],

time: 210 us -> 207 us (0.986)
  Pallas kernels: 208 us -> 205 us
    pallas_call x1, Pallas kernels: 208 us -> 205 us  [local(): pl.pallas_call(functools.partial(kernel, dims), out_shape=jax.ShapeDtypeS...]
where the time goes in v3:
time: 207 us
  Pallas kernels  205 us (99%)
    pallas_call x1, Pallas kernels, local(): pl.pallas_call(functools.partial(kernel, dims), out_shape=jax.ShapeDtypeS...  205 us

profile of v3, /device:TPU:0, one launch (start us, length us, event | category | flops | bytes accessed | tf_op | source)
XLA Modules:
  0.0 207.2 jit_solution(11655713399657430222)
XLA Ops:
  0.0 205.3 %shard_map.46 = f32[16,8192]{1,0:T(8,128)} custom-call(bf16[512,8192]{1,0:T(8,128)(2,1)} %bitcast.2, bf16[128,8192]{1,0:T(8,128)(2,1)} %bitcast.3, s32[8,512]{1,0:T(8,128)} %flags.1, s32[256,256]{1,0:T(8,128)} %ticks.1), custom_call_target="tpu_custom_call" | custom-call | tf_op jit(solution)/shard_map/pallas_call | solution.py:234
  205.3 1.9 copy.6
